TPU v7x, 256 devices: a whole 4x4x8 slice. The times are simulated.
256 devices in a mesh: head: 8 (over y, x_lo), tok: 32 (over x_hi, z, core).
Axes of the slice: x: 4 (x_hi: 2, x_lo: 2; x = x_hi * 2 + x_lo), y: 4, z: 8, core: 2. Of those that a mesh axis runs over, the one named last changes fastest.
Arguments:
- head_outputs: bfloat16 [1024, 8192], P('tok', 'head'), may hold values from -6 to 6
- dec_bias: float32 [8192], P('head'), may hold values from -3 to 3
- enc_bias: float32 [65536], P('tok'), may hold values from -3 to 3
- enc_weight: bfloat16 [8192, 65536], P('head', 'tok'), may hold values from -0.0625 to 0.0625
- dec_weight: bfloat16 [65536, 8192], P('tok', 'head'), may hold values from -0.75 to 0.75
- out_weight: bfloat16 [8192, 8192], P('head', 'tok'), may hold values from -0.0625 to 0.0625
- active_ids: int32 [1024, 128], replicated, may hold values from 0 to 65535, as said below
Outputs:
- reconstruction: bfloat16 [1024, 8192], P('tok', 'head')
- projected: bfloat16 [1024, 8192], P('tok', 'head')
Inputs may be any that keep to these rules, and one draw needn't show every extreme that they name: `active_ids`: entry j of each row lies among the latents j * 512 to (j + 1) * 512 - 1, so the 128 entries of a row are different.
All inputs are finite; a program needn't handle non-finite values.
Results may differ from a plain program's by a relative error of at most 0.0061.
Values may be sent and summed in bfloat16 or wider, within the bound.
A program may use at most 128 MiB of HBM per device.

v0:
```python
import jax
import jax.numpy as jnp
from jax import lax
from jax.sharding import PartitionSpec as P


def latent_mask(id_rows, lat_start, lat_count):
    row_count = id_rows.shape[0]
    shifted = id_rows - lat_start
    inside = (shifted >= 0) & (shifted < lat_count)
    shifted = jnp.where(inside, shifted, lat_count)
    row_ids = jnp.arange(row_count, dtype=jnp.int32)[:, None]
    return jnp.zeros((row_count, lat_count), jnp.float32).at[row_ids, shifted].set(1.0, mode="drop")


def dense_decoder(latents, dec_weight):

    def decode(start, count):
        return jnp.dot(latents, dec_weight, preferred_element_type=jnp.float32)

    return decode


def on_device(head_outputs, dec_bias, enc_bias, enc_weight, dec_weight, out_weight, active_ids):
    centered = (head_outputs.astype(jnp.float32) - dec_bias[None, :]).astype(jnp.bfloat16)
    lat_count = enc_weight.shape[1]
    lat_start = lax.axis_index("tok") * lat_count
    partial_pre = jnp.dot(
        lax.all_gather(centered, "tok", axis=0, tiled=True),
        enc_weight,
        preferred_element_type=jnp.float32,
    )
    pre = lax.psum(partial_pre, "head") + enc_bias[None, :]
    mask = latent_mask(active_ids, lat_start, lat_count)
    latents = (mask * jnp.maximum(pre, 0.0)).astype(jnp.bfloat16)
    decode = dense_decoder(latents, dec_weight)
    decoded = lax.psum_scatter(
        decode(jnp.int32(0), head_outputs.shape[0] * lax.axis_size("tok")),
        "tok",
        scatter_dimension=0,
        tiled=True,
    )
    reconstruction = (decoded + dec_bias[None, :]).astype(jnp.bfloat16)
    partial_out = jnp.dot(
        reconstruction,
        lax.all_gather(out_weight, "tok", axis=1, tiled=True),
        preferred_element_type=jnp.float32,
    )
    projected = lax.psum_scatter(partial_out, "head", scatter_dimension=1, tiled=True).astype(
        jnp.bfloat16
    )
    return (reconstruction, projected)


def solution(mesh):
    return jax.shard_map(
        on_device,
        mesh=mesh,
        in_specs=(
            P("tok", "head"),
            P("head"),
            P("tok"),
            P("head", "tok"),
            P("tok", "head"),
            P("head", "tok"),
            P(),
        ),
        out_specs=(P("tok", "head"), P("tok", "head")),
        check_vma=False,
    )
```

profile of v0, /device:TPU:4, one launch (start us, length us, event | category | flops | bytes accessed | tf_op | source)
XLA Modules:
  0.0 947.2 jit_solution(17735549942467260121)
XLA Ops:
  7.2 0.0 all-gather.3.cloned.1.call-start
  7.2 1.5 subtract_convert_fusion
  8.7 0.0 all-gather.3.cloned.1.call-update
  8.7 0.0 all-reduce.2.cloned.1.call-start
  8.8 83.0 %all-gather.3.cloned.1.call-done = bf16[1024,1024]{1,0:T(8,128)(2,1)} async-done(((bf16[32,1024]{1,0:T(8,128)(2,1)}), bf16[1024,1024]{1,0:T(8,128)(2,1)}) %all-gather.3.cloned.1.call-update) | async-done | bytes 2097168 | tf_op jit(solution)/shard_map/all_gather | solution.py:29
  91.8 10.5 %fusion.7 = f32[1024,2048]{1,0:T(8,128)} fusion(bf16[1024,1024]{1,0:T(8,128)(2,1)} %all-gather.3.cloned.1.call-done, bf16[1024,2048]{1,0:T(8,128)(2,1)} %param.10), kind=kOutput, calls=%fused_computation.16 | convolution fusion | flops 4294967296 | bytes 14680064 | tf_op jit(solution)/shard_map/dot_general | solution.py:28
  102.3 0.0 copy-start
  102.3 0.0 copy-start.4
  102.3 0.0 copy-start.3
  102.4 0.0 all-reduce.2.cloned.1.call-update
  102.4 0.0 reduce-scatter.3.cloned.1.call-start
  102.4 1.0 copy-done
  103.4 0.1 fusion.5
  103.6 0.0 copy-done.4
  103.6 0.1 multiply_reduce_fusion
  103.7 0.0 copy-done.3
  103.7 0.3 and_reduce_fusion
  104.0 0.1 select_bitcast_fusion
  104.1 482.1 %scatter_custom_fusion = f32[2097152]{0:T(1024)} fusion(s32[131072]{0:T(1024)S(1)} %select_bitcast_fusion, f32[131072]{0:T(1024)S(1)} %broadcast.26, f32[]{:T(128)} %constant.5.clone.1), kind=kCustom, calls=%fused_computation.3 | custom fusion | bytes 8388612
  586.2 0.0 copy-start.5
  586.2 9.3 reshape.11
  595.5 0.0 copy-start.2
  595.5 0.0 all-reduce.2.cloned.1.call-done
  595.5 0.0 copy-done.5
  595.5 13.4 %fusion = f32[1024,1024]{1,0:T(8,128)} fusion(bf16[2048,1024]{1,0:T(8,128)(2,1)} %param.11, f32[1024,2048]{1,0:T(8,128)} %reshape.11, f32[1024,2048]{1,0:T(8,128)} %all-reduce.2.cloned.1.call-done, f32[2048]{0:T(1024)S(1)} %copy-done.5), kind=kOutput, calls=%fused_computation.2 | convolution fusion | flops 4303355904 | bytes 25174016 | tf_op jit(solution)/shard_map/dot_general | solution.py:19
  608.9 0.0 reduce-scatter.3.cloned.1.call-update
  608.9 0.0 all-gather.5.cloned.1.call-start
  608.9 0.5 all-gather.5.cloned.1.call-update
  609.5 0.2 reduce-scatter.5.cloned.1.call-start
  609.7 125.0 %reduce-scatter.3.cloned.1.call-done = f32[32,1024]{1,0:T(8,128)} async-done(((f32[1024,1024]{1,0:T(8,128)}), f32[32,1024]{1,0:T(8,128)}) %reduce-scatter.3.cloned.1.call-update) | async-done | bytes 131088 | tf_op jit(solution)/shard_map/reduce_scatter | solution.py:37
  734.7 0.0 copy-done.2
  734.7 0.9 add_convert_fusion
  735.7 0.0 copy-start.1
  735.7 152.1 %all-gather.5.cloned.1.call-done = bf16[1024,8192]{1,0:T(8,128)(2,1)} async-done(((bf16[1024,256]{1,0:T(8,128)(2,1)}), bf16[1024,8192]{1,0:T(8,128)(2,1)}) %all-gather.5.cloned.1.call-update) | async-done | bytes 16777232 | tf_op jit(solution)/shard_map/all_gather | solution.py:46
  887.8 9.7 %fusion.8 = f32[32,8192]{1,0:T(8,128)} fusion(bf16[32,1024]{1,0:T(8,128)(2,1)S(1)} %add_convert_fusion, bf16[1024,8192]{1,0:T(8,128)(2,1)} %all-gather.5.cloned.1.call-done), kind=kOutput, calls=%fused_computation.17 | convolution fusion | flops 536870912 | bytes 17891328 | tf_op jit(solution)/shard_map/dot_general | solution.py:44
  897.5 0.0 copy-done.1
  897.5 0.0 reduce-scatter.5.cloned.1.call-update
  897.5 41.6 %reduce-scatter.5.cloned.1.call-done = f32[32,1024]{1,0:T(8,128)} async-done(((f32[32,8192]{1,0:T(8,128)}), f32[32,1024]{1,0:T(8,128)}) %reduce-scatter.5.cloned.1.call-update) | async-done | bytes 131088 | tf_op jit(solution)/shard_map/reduce_scatter | solution.py:49
  939.1 1.5 convert_element_type.19
  (2 shorter events, 0.1 us)
Async XLA Ops:
  7.2 84.6 %all-gather.3.cloned.1.call-start = ((), (), s32[]{:S(2)}) async-start(), calls=%async_computation.2 | async-start | bytes 2162688 | tf_op jit(solution)/shard_map/all_gather | solution.py:29
  8.7 586.7 %all-reduce.2.cloned.1.call-start = ((), (), s32[]{:S(2)}) async-start(), calls=%async_computation.3 | async-start | bytes 16777216 | tf_op jit(solution)/shard_map/psum | solution.py:33
  102.3 1.0 copy-start
  102.3 1.2 copy-start.4
  102.3 1.4 copy-start.3
  102.4 632.4 %reduce-scatter.3.cloned.1.call-start = ((), (), s32[]{:S(2)}) async-start(), calls=%async_computation.4 | async-start | bytes 4325376 | tf_op jit(solution)/shard_map/reduce_scatter | solution.py:37
  586.2 9.3 copy-start.5
  595.5 139.3 %copy-start.2 = (f32[1024]{0:T(1024)S(1)}, f32[1024]{0:T(1024)}, u32[]{:S(2)}) copy-start(f32[1024]{0:T(1024)} %param.8) | copy-start | bytes 12292
  608.9 278.9 %all-gather.5.cloned.1.call-start = ((), (), s32[]{:S(2)}) async-start(), calls=%async_computation.5 | async-start | bytes 17301504 | tf_op jit(solution)/shard_map/all_gather | solution.py:46
  609.5 329.7 %reduce-scatter.5.cloned.1.call-start = ((), (), s32[]{:S(2)}) async-start(), calls=%async_computation.6 | async-start | bytes 1179648 | tf_op jit(solution)/shard_map/reduce_scatter | solution.py:49
  735.7 161.9 %copy-start.1 = (bf16[32,1024]{1,0:T(8,128)(2,1)}, bf16[32,1024]{1,0:T(8,128)(2,1)S(1)}, u32[]{:S(2)}) copy-start(bf16[32,1024]{1,0:T(8,128)(2,1)S(1)} %add_convert_fusion) | copy-start | bytes 196612
Sparse Core Ops, SparseCore 0:
  11.3 80.4 all-gather.2
  102.5 343.3 all-reduce.1
  609.0 125.6 reduce-scatter.2
  737.5 150.2 all-gather.4
  897.7 41.4 reduce-scatter.4
where the time goes:
time: 948 us; the launch traced here: 947 us
  local copies, waits for them, and re-layouts  492 us (52%)
  waiting for transfers between devices  402 us (42%)
  matrix products  33.7 us (4%)
  between operations  13.8 us (1%)
    unnamed x14, local copies, waits for them, and re-layouts  483 us
    all_gather x1, waiting for transfers between devices, on_device(): lax.all_gather(out_weight, 'tok', axis=1, tiled=True)  152 us
    reduce_scatter x1, waiting for transfers between devices, on_device(): lax.psum_scatter(decode(jnp.int32(0), head_outputs.shape[0] * lax.axis_si...  125 us
    all_gather x1, waiting for transfers between devices, on_device(): lax.all_gather(centered, 'tok', axis=0, tiled=True)  83 us
    reduce_scatter x1, waiting for transfers between devices, on_device(): lax.psum_scatter(partial_out, 'head', scatter_dimension=1, tiled=True)  41.6 us
  transfers between devices with their start and end apart: 5, of which 4 were waited for; matrix products, arithmetic and copies ran while one was open for 52% of the time, Pallas kernels for 0%

commit v1 on v0

--- a/solution.py
+++ b/solution.py
@@ -43,7 +43,9 @@
     reconstruction = (decoded + dec_bias[None, :]).astype(jnp.bfloat16)
     partial_out = jnp.dot(
         reconstruction,
-        lax.all_gather(out_weight, "tok", axis=1, tiled=True),
+        jnp.concatenate(
+            lax.all_to_all(jnp.stack([out_weight] * lax.axis_size("tok")), "tok", 0, 0), axis=1
+        ),
         preferred_element_type=jnp.float32,
     )
     projected = lax.psum_scatter(partial_out, "head", scatter_dimension=1, tiled=True).astype(

time: 948 us -> 868 us (0.916)
  waiting for transfers between devices: 402 us -> 303 us
  starting transfers between devices: 0.38 us -> 12.1 us
    all_gather x1 -> x0, waiting for transfers between devices: 152 us -> none  [on_device(): lax.all_gather(out_weight, 'tok', axis=1, tiled=True)]
    all_gather x1, waiting for transfers between devices: 83 us -> 132 us  [on_device(): lax.all_gather(centered, 'tok', axis=0, tiled=True)]
    all_to_all x0 -> x1, starting transfers between devices: none -> 11.8 us  [on_device(): lax.all_to_all(jnp.stack([out_weight] * lax.axis_size('tok')), 'tok', 0, 0)]
    unnamed x14 -> x17, local copies, waits for them, and re-layouts: 483 us -> 484 us
  transfers between devices with their start and end apart: 5 -> 5, of which waited for: 4 -> 3; matrix products, arithmetic and copies ran while one was open for 52% -> 60% of each run, Pallas kernels for 0% -> 0%
where the time goes in v1:
time: 868 us; the launch traced here: 867 us
  local copies, waits for them, and re-layouts  500 us (58%)
  waiting for transfers between devices  303 us (35%)
  matrix products  35.7 us (4%)
  between operations  13.9 us (2%)
  starting transfers between devices  12.1 us (1%)
    unnamed x17, local copies, waits for them, and re-layouts  484 us
    all_gather x1, waiting for transfers between devices, on_device(): lax.all_gather(centered, 'tok', axis=0, tiled=True)  132 us
    reduce_scatter x1, waiting for transfers between devices, on_device(): lax.psum_scatter(decode(jnp.int32(0), head_outputs.shape[0] * lax.axis_si...  128 us
    reduce_scatter x1, waiting for transfers between devices, on_device(): lax.psum_scatter(partial_out, 'head', scatter_dimension=1, tiled=True)  42.9 us
  transfers between devices with their start and end apart: 5, of which 3 were waited for; matrix products, arithmetic and copies ran while one was open for 60% of the time, Pallas kernels for 0%

profile of v1, /device:TPU:4, one launch (start us, length us, event | category | flops | bytes accessed | tf_op | source)
XLA Modules:
  0.0 867.5 jit_solution(17155444715181003260)
XLA Ops:
  7.2 1.2 copy.9
  8.4 6.0 stack.2
  14.4 0.0 copy-start.2
  14.4 0.0 copy-start.3
  14.4 11.8 %all-to-all-start = ((bf16[32,1024,256]{1,2,0:T(8,128)(2,1)}), bf16[32,1024,256]{1,2,0:T(8,128)(2,1)}, u32[]{:S(2)}, u32[]{:S(2)}) async-start(bf16[32,1024,256]{1,2,0:T(8,128)(2,1)} %stack.2), calls=%async_computation.1 | async-start | bytes 33554432 | tf_op jit(solution)/shard_map/all_to_all | solution.py:47
  26.2 0.0 all-gather.2.cloned.1.call-start
  26.3 0.0 copy-done.2
  26.3 0.0 copy-done.3
  26.3 0.6 subtract_convert_fusion
  26.9 0.0 all-gather.2.cloned.1.call-update
  26.9 0.0 all-reduce.2.cloned.1.call-start
  27.0 132.0 %all-gather.2.cloned.1.call-done = bf16[1024,1024]{1,0:T(8,128)(2,1)} async-done(((bf16[32,1024]{1,0:T(8,128)(2,1)}), bf16[1024,1024]{1,0:T(8,128)(2,1)}) %all-gather.2.cloned.1.call-update) | async-done | bytes 2097168 | tf_op jit(solution)/shard_map/all_gather | solution.py:29
  159.0 10.5 %fusion.7 = f32[1024,2048]{1,0:T(8,128)} fusion(bf16[1024,1024]{1,0:T(8,128)(2,1)} %all-gather.2.cloned.1.call-done, bf16[1024,2048]{1,0:T(8,128)(2,1)} %param.10), kind=kOutput, calls=%fused_computation.16 | convolution fusion | flops 4294967296 | bytes 14680064 | tf_op jit(solution)/shard_map/dot_general | solution.py:28
  169.5 0.0 copy-start
  169.5 0.0 copy-start.5
  169.5 0.0 copy-start.4
  169.5 0.0 all-reduce.2.cloned.1.call-update
  169.5 0.0 reduce-scatter.3.cloned.1.call-start
  169.6 1.0 copy-done
  170.6 0.1 fusion.5
  170.7 0.0 copy-done.5
  170.7 0.1 multiply_reduce_fusion
  170.9 0.0 copy-done.4
  170.9 0.3 and_reduce_fusion
  171.2 0.1 select_bitcast_fusion
  171.3 482.1 %scatter_custom_fusion = f32[2097152]{0:T(1024)} fusion(s32[131072]{0:T(1024)S(1)} %select_bitcast_fusion, f32[131072]{0:T(1024)S(1)} %broadcast.28, f32[]{:T(128)} %constant.5.clone.1), kind=kCustom, calls=%fused_computation.3 | custom fusion | bytes 8388612
  653.3 0.0 copy-start.6
  653.4 9.2 %reshape.21 = f32[1024,2048]{1,0:T(8,128)} reshape(f32[2097152]{0:T(1024)} %scatter_custom_fusion) | data formatting | bytes 16777216 | tf_op jit(solution)/shard_map/scatter | solution.py:13
  662.6 0.0 all-reduce.2.cloned.1.call-done
  662.6 0.0 copy-done.6
  662.6 13.4 %fusion = f32[1024,1024]{1,0:T(8,128)} fusion(bf16[2048,1024]{1,0:T(8,128)(2,1)} %param.11, f32[1024,2048]{1,0:T(8,128)} %reshape.21, f32[1024,2048]{1,0:T(8,128)} %all-reduce.2.cloned.1.call-done, f32[2048]{0:T(1024)S(1)} %copy-done.6), kind=kOutput, calls=%fused_computation.2 | convolution fusion | flops 4303355904 | bytes 25174016 | tf_op jit(solution)/shard_map/dot_general | solution.py:19
  676.0 0.0 reduce-scatter.3.cloned.1.call-update
  676.0 0.2 reduce-scatter.5.cloned.1.call-start
  676.2 127.6 %reduce-scatter.3.cloned.1.call-done = f32[32,1024]{1,0:T(8,128)} async-done(((f32[1024,1024]{1,0:T(8,128)}), f32[32,1024]{1,0:T(8,128)}) %reduce-scatter.3.cloned.1.call-update) | async-done | bytes 131088 | tf_op jit(solution)/shard_map/reduce_scatter | solution.py:37
  803.8 0.9 add_convert_fusion
  804.7 0.0 copy-start.1
  804.7 0.0 all-to-all-done
  804.7 11.8 %fusion.8 = f32[32,8192]{1,0:T(8,128)} fusion(bf16[32,1024]{1,0:T(8,128)(2,1)S(1)} %add_convert_fusion, bf16[1024,8192]{0,1:T(8,128)(2,1)} %bitcast.3), kind=kOutput, calls=%fused_computation.17 | convolution fusion | flops 536870912 | bytes 17891328 | tf_op jit(solution)/shard_map/dot_general | solution.py:44
  816.5 0.0 copy-done.1
  816.5 0.0 reduce-scatter.5.cloned.1.call-update
  816.5 42.9 %reduce-scatter.5.cloned.1.call-done = f32[32,1024]{1,0:T(8,128)} async-done(((f32[32,8192]{1,0:T(8,128)}), f32[32,1024]{1,0:T(8,128)}) %reduce-scatter.5.cloned.1.call-update) | async-done | bytes 131088 | tf_op jit(solution)/shard_map/reduce_scatter | solution.py:51
  859.4 1.5 convert_element_type.19
  (2 shorter events, 0.1 us)
Async XLA Ops:
  14.4 11.8 %copy-start.2 = (bf16[32,1024]{1,0:T(8,128)(2,1)S(1)}, bf16[32,1024]{1,0:T(8,128)(2,1)}, u32[]{:S(2)}) copy-start(bf16[32,1024]{1,0:T(8,128)(2,1)} %param.7) | copy-start | bytes 196612
  14.4 11.9 %copy-start.3 = (f32[1024]{0:T(1024)S(1)}, f32[1024]{0:T(1024)}, u32[]{:S(2)}) copy-start(f32[1024]{0:T(1024)} %param.8) | copy-start | bytes 12292
  14.4 790.3 %all-to-all-start = ((bf16[32,1024,256]{1,2,0:T(8,128)(2,1)}), bf16[32,1024,256]{1,2,0:T(8,128)(2,1)}, u32[]{:S(2)}, u32[]{:S(2)}) async-start(bf16[32,1024,256]{1,2,0:T(8,128)(2,1)} %stack.2), calls=%async_computation.1 | async-start | bytes 33554432 | tf_op jit(solution)/shard_map/all_to_all | solution.py:47
  26.2 132.8 %all-gather.2.cloned.1.call-start = ((), (), s32[]{:S(2)}) async-start(), calls=%async_computation.3 | async-start | bytes 2162688 | tf_op jit(solution)/shard_map/all_gather | solution.py:29
  26.9 635.7 %all-reduce.2.cloned.1.call-start = ((), (), s32[]{:S(2)}) async-start(), calls=%async_computation.4 | async-start | bytes 16777216 | tf_op jit(solution)/shard_map/psum | solution.py:33
  169.5 1.0 copy-start
  169.5 1.2 copy-start.5
  169.5 1.4 copy-start.4
  169.5 634.3 %reduce-scatter.3.cloned.1.call-start = ((), (), s32[]{:S(2)}) async-start(), calls=%async_computation.5 | async-start | bytes 4325376 | tf_op jit(solution)/shard_map/reduce_scatter | solution.py:37
  653.3 9.3 %copy-start.6 = (f32[2048]{0:T(1024)S(1)}, f32[2048]{0:T(1024)}, u32[]{:S(2)}) copy-start(f32[2048]{0:T(1024)} %param.9) | copy-start | bytes 24580
  676.0 183.4 %reduce-scatter.5.cloned.1.call-start = ((), (), s32[]{:S(2)}) async-start(), calls=%async_computation.6 | async-start | bytes 1179648 | tf_op jit(solution)/shard_map/reduce_scatter | solution.py:51
  804.7 11.8 %copy-start.1 = (bf16[32,1024]{1,0:T(8,128)(2,1)}, bf16[32,1024]{1,0:T(8,128)(2,1)S(1)}, u32[]{:S(2)}) copy-start(bf16[32,1024]{1,0:T(8,128)(2,1)S(1)} %add_convert_fusion) | copy-start | bytes 196612
Sparse Core Ops, SparseCore 0:
  30.4 128.5 all-gather.1
  169.7 444.9 all-reduce.1
  676.1 127.6 reduce-scatter.2
  816.7 42.7 reduce-scatter.4
